TPU v7x, 32 devices: a whole 2x2x4 slice. The times are simulated.
32 devices in a mesh: grp: 2 (over y), energy: 4 (over z), atom: 2 (over x), kz: 2 (over core).
Axes of the slice: x: 2, y: 2, z: 4, core: 2. Of those that a mesh axis runs over, the one named last changes fastest.
Arguments:
- green: float32 [8, 32, 512, 512], P(('grp', 'kz'), 'energy', 'atom'), parts along dimension 0, may hold values from -6 to 6
- couplings: float32 [4, 512, 512], P('atom'), may hold values from -0.25 to 0.25
- occupation: float32 [3], replicated, may hold values from 0.05 to 2
- offsets: int32 [3], replicated, may hold values from 1 to 16, as said below
- owners: int32 [3], replicated, may hold values from 0 to 3
Outputs:
- sigma: float32 [1024, 32, 512], P(('grp', 'atom', 'kz'), 'energy'), parts along dimension 0
There are 2 independent parts, one for each index of `grp`. A program takes and returns all parts, laid end to end along the dimension named above; an argument that names none is the same for every part. Nothing has to cross between parts.
Inputs may be any that keep to these rules, and one draw needn't show every extreme that they name: `offsets`: one mode's offset is exactly 16.
All inputs are finite; a program needn't handle non-finite values.
Results may differ from a plain program's by a relative error of at most 0.0001.
Values sent between devices are 32-bit elements; how exact they have to be, the bound alone decides.
A program may use at most 192 MiB of HBM per device.

v0:
```python
import jax
import jax.numpy as jnp
from jax import lax
from jax.sharding import PartitionSpec as P

MODES = 3


def broadcast(array, axis, root):
    mine = lax.axis_index(axis) == root
    return lax.psum(jnp.where(mine, array, jnp.zeros_like(array)), axis)


def shards(green, couplings, occupation, offsets, owners):
    momenta_here, edev, brows, order = green.shape
    momenta = momenta_here * lax.axis_size("kz")
    source = jnp.sum(green, axis=0)
    gathered = lax.all_gather(source, "energy", axis=0, tiled=True)
    grid_total = gathered.shape[0]
    place = lax.axis_index("energy")
    picks = (place * edev + jnp.arange(-2 * edev, 3 * edev, dtype=jnp.int32)) % grid_total
    window = jnp.take(gathered, picks, axis=0)
    row_first = lax.axis_index("atom") * brows
    table_rows = couplings.shape[0]
    matrices = []
    products = []
    for mode in range(MODES):
        owner = owners[mode]
        local = lax.dynamic_index_in_dim(couplings, owner % table_rows, 0, keepdims=False)
        coupling = broadcast(local, "atom", owner // table_rows)
        step = offsets[mode]
        upper = lax.dynamic_slice_in_dim(window, 2 * edev + step, edev, 0)
        lower = lax.dynamic_slice_in_dim(window, 2 * edev - step, edev, 0)
        weight = occupation[mode]
        combined = ((1.0 + weight) * upper + weight * lower) / momenta
        product = jnp.einsum("eac,dc->ead", combined, coupling, precision=lax.Precision.HIGHEST)
        matrices.append(coupling)
        products.append(product)
    rows_out = order // (lax.axis_size("atom") * lax.axis_size("kz"))
    total = jnp.zeros((rows_out * lax.axis_size(("atom", "kz")), edev, order), jnp.float32)
    for coupling, product in zip(matrices, products):
        block = lax.dynamic_slice(
            coupling, (0, row_first), (rows_out * lax.axis_size(("atom", "kz")), brows)
        )
        total = total + jnp.einsum("ra,ead->red", block, product, precision=lax.Precision.HIGHEST)
    return lax.psum_scatter(total, ("atom", "kz"), scatter_dimension=0, tiled=True)


def solution(mesh):
    return jax.shard_map(
        shards,
        mesh=mesh,
        in_specs=(P(("grp", "kz"), "energy", "atom", None), P("atom", None, None), P(), P(), P()),
        out_specs=P(("grp", "atom", "kz"), "energy", None),
        check_vma=False,
    )
```

profile of v0, /device:TPU:0, one launch (start us, length us, event | category | flops | bytes accessed | tf_op | source)
XLA Modules:
  0.0 477.6 jit_solution(8491351570519388866)
XLA Ops:
  7.4 6.8 %reduce_sum.9 = f32[8,256,512]{2,1,0:T(8,128)} reduce(f32[2,8,256,512]{3,2,1,0:T(8,128)} %param.5, f32[]{:T(128)} %constant.119.clone.1), dimensions={0}, to_apply=%region_1.2 | reduce | flops 1048576 | bytes 12582916 | tf_op jit(solution)/shard_map/reduce_sum | solution.py:17
  14.2 0.0 all-gather.2.cloned.1.call-update
  14.2 0.0 all-reduce.3.cloned.1.call-start
  14.2 0.6 copy-done.4
  14.8 0.6 fusion.55
  23.0 0.0 copy-start.5
  23.0 0.0 copy-start.6
  23.0 1.8 select_bitcast_fusion
  24.8 0.0 all-reduce.3.cloned.1.call-update
  24.8 0.0 reduce-scatter.2.cloned.1.call-start
  24.9 0.7 fusion.54
  33.6 0.6 fusion.53
  36.1 267.8 %all-gather.2.cloned.1.call-done = f32[32,256,512]{2,1,0:T(8,128)} async-done(((f32[8,256,512]{2,1,0:T(8,128)}), f32[32,256,512]{2,1,0:T(8,128)}) %all-gather.2.cloned.1.call-update) | async-done | bytes 16777232 | tf_op jit(solution)/shard_map/all_gather | solution.py:18
  303.9 15.3 %gather_fusion = f32[40,256,512]{2,1,0:T(8,128)} fusion(f32[32,256,512]{2,1,0:T(8,128)} %all-gather.2.cloned.1.call-done, s32[1024]{0:T(1024)S(1)} %pad_clamp_fusion), kind=kCustom, calls=%fused_computation | custom fusion | bytes 41943200 | tf_op jit(solution)/shard_map/jit(_take)/gather | solution.py:22
  319.2 16.8 %broadcast_select_fusion = f32[40,256,512]{2,1,0:T(8,128)} fusion(f32[40,256,512]{2,1,0:T(8,128)} %gather_fusion, pred[40]{0:T(512)(128)(4,1)S(1)} %compare_and_fusion), kind=kLoop, calls=%fused_computation.1 | loop fusion | flops 5242880 | bytes 41943080 | tf_op jit(solution)/shard_map/jit(_take)/select_n | solution.py:22
  335.9 10.9 %fusion.7 = f32[8,256,512]{2,1,0:T(8,128)S(1)} fusion(f32[40,256,512]{2,1,0:T(8,128)} %broadcast_select_fusion, s32[]{:T(128)S(6)} %select_n.145, s32[]{:T(128)S(6)} %select_n.144, f32[]{:T(128)} %bitcast.13, f32[]{:T(128)S(6)} %add.217, f32[512,512]{1,0:T(8,128)} %get-tuple-element.6), kind=kOutput, calls=%fused_computation.10 | convolution fusion | flops 6446645248 | bytes 13632012 | tf_op jit(solution)/shard_map/eac,dc->ead/dot_general | solution.py:36
  346.9 8.0 %fusion.34 = f32[512,8,512]{2,0,1:T(8,128)S(1)} fusion(f32[8,256,512]{2,1,0:T(8,128)S(1)} %fusion.7, f32[512,512]{1,0:T(8,128)} %get-tuple-element.6, s32[]{:T(128)S(6)} %select_n.130), kind=kOutput, calls=%fused_computation.40 | convolution fusion | flops 6442450944 | bytes 13107204 | tf_op jit(solution)/shard_map/ra,ead->red/dot_general | solution.py:45
  354.9 9.3 %fusion.14 = f32[8,256,512]{2,1,0:T(8,128)} fusion(f32[40,256,512]{2,1,0:T(8,128)S(1)} %copy-done, s32[]{:T(128)S(6)} %select_n.137, s32[]{:T(128)S(6)} %select_n.136, f32[]{:T(128)} %bitcast.3, f32[]{:T(128)S(6)} %add.195, f32[512,512]{1,0:T(8,128)S(1)} %copy-done.3), kind=kOutput, calls=%fused_computation.17 | convolution fusion | flops 6446645248 | bytes 13631504 | tf_op jit(solution)/shard_map/eac,dc->ead/dot_general | solution.py:36
  364.2 10.8 %fusion.36 = f32[512,8,512]{2,0,1:T(8,128)S(1)} fusion(f32[8,256,512]{2,1,0:T(8,128)} %fusion.14, f32[512,512]{1,0:T(8,128)S(1)} %copy-done.3, s32[]{:T(128)S(6)} %select_n.130), kind=kOutput, calls=%fused_computation.42 | convolution fusion | flops 6442450944 | bytes 13107204 | tf_op jit(solution)/shard_map/ra,ead->red/dot_general | solution.py:45
  375.0 9.3 %fusion = f32[8,256,512]{2,1,0:T(8,128)} fusion(f32[40,256,512]{2,1,0:T(8,128)S(1)} %copy-done, s32[]{:T(128)S(6)} %select_n.153, s32[]{:T(128)S(6)} %select_n.152, f32[]{:T(128)} %bitcast.22, f32[]{:T(128)S(6)} %add.228, f32[512,512]{1,0:T(8,128)S(1)} %copy-done.2), kind=kOutput, calls=%fused_computation.3 | convolution fusion | flops 6446645248 | bytes 13631504 | tf_op jit(solution)/shard_map/eac,dc->ead/dot_general | solution.py:36
  384.3 11.8 %add_add_fusion = f32[512,8,512]{2,0,1:T(8,128)} fusion(f32[512,8,512]{2,0,1:T(8,128)S(1)} %fusion.36, f32[512,8,512]{2,0,1:T(8,128)S(1)} %fusion.34, f32[8,256,512]{2,1,0:T(8,128)} %fusion, f32[512,512]{1,0:T(8,128)S(1)} %copy-done.2, s32[]{:T(128)S(6)} %select_n.130), kind=kOutput, calls=%fused_computation.2 | convolution fusion | flops 6446645248 | bytes 29884420 | tf_op jit(solution)/shard_map/ra,ead->red/dot_general | solution.py:45
  396.1 0.0 reduce-scatter.2.cloned.1.call-update
  396.1 69.9 %reduce-scatter.2.cloned.1.call-done = f32[128,8,512]{2,0,1:T(8,128)} async-done(((f32[512,8,512]{2,0,1:T(8,128)}), f32[128,8,512]{2,0,1:T(8,128)}) %reduce-scatter.2.cloned.1.call-update) | async-done | bytes 2097168 | tf_op jit(solution)/shard_map/reduce_scatter | solution.py:46
  466.0 4.1 copy.7
  (16 shorter events, 0.1 us)
Async XLA Ops:
  7.4 296.5 %all-gather.2.cloned.1.call-start = ((), (), s32[]{:S(2)}) async-start(), calls=%async_computation.1 | async-start | bytes 20971520 | tf_op jit(solution)/shard_map/all_gather | solution.py:18
  14.2 0.7 copy-start.4
  14.2 8.8 %copy-start.1 = (f32[2,512,512]{2,1,0:T(8,128)S(1)}, f32[2,512,512]{2,1,0:T(8,128)}, u32[]{:S(2)}) copy-start(f32[2,512,512]{2,1,0:T(8,128)} %param.6) | copy-start | bytes 6291460
  14.2 321.8 %all-reduce.3.cloned.1.call-start = ((), (), s32[]{:S(2)}) async-start(), calls=%async_computation.3 | async-start | bytes 6291456 | tf_op jit(solution)/shard_map/psum | solution.py:11
  23.0 1.9 copy-start.5
  23.0 10.5 %copy-start.6 = (f32[3]{0:T(128)S(1)}, f32[3]{0:T(128)}, u32[]{:S(2)}) copy-start(f32[3]{0:T(128)} %param.7) | copy-start | bytes 40
  24.8 441.2 %reduce-scatter.2.cloned.1.call-start = ((), (), s32[]{:S(2)}) async-start(), calls=%async_computation.2 | async-start | bytes 10485760 | tf_op jit(solution)/shard_map/reduce_scatter | solution.py:46
  335.9 19.0 %copy-start = (f32[40,256,512]{2,1,0:T(8,128)S(1)}, f32[40,256,512]{2,1,0:T(8,128)}, u32[]{:S(2)}) copy-start(f32[40,256,512]{2,1,0:T(8,128)} %broadcast_select_fusion) | copy-start | bytes 62914564
  346.9 8.0 %copy-start.3 = (f32[512,512]{1,0:T(8,128)S(1)}, f32[512,512]{1,0:T(8,128)}, u32[]{:S(2)}) copy-start(f32[512,512]{1,0:T(8,128)} %get-tuple-element.5) | copy-start | bytes 3145732
  364.2 10.8 %copy-start.2 = (f32[512,512]{1,0:T(8,128)S(1)}, f32[512,512]{1,0:T(8,128)}, u32[]{:S(2)}) copy-start(f32[512,512]{1,0:T(8,128)} %get-tuple-element.7) | copy-start | bytes 3145732
Sparse Core Ops, SparseCore 0:
  14.3 289.4 all-gather.1
Sparse Core Ops, SparseCore 1:
  24.9 88.7 all-reduce.2
  396.2 69.8 reduce-scatter.1
where the time goes:
time: 478 us
  waiting for transfers between devices  338 us (71%)
  matrix products  60.1 us (13%)
  between operations  32.4 us (7%)
  other arithmetic  25.4 us (5%)
  local copies, waits for them, and re-layouts  21.9 us (5%)
    all_gather x1, waiting for transfers between devices, shards(): gathered = lax.all_gather(source, 'energy', axis=0, tiled=True)  268 us
    reduce_scatter x1, waiting for transfers between devices, shards(): lax.psum_scatter(total, ('atom', 'kz'), scatter_dimension=0, tiled=True)  69.9 us
    dot_general x3, matrix products, shards(): jnp.einsum('ra,ead->red', block, product, precision=lax.Precision.HIGHEST)  30.5 us
    dot_general x3, matrix products, shards(): jnp.einsum('eac,dc->ead', combined, coupling, precision=lax.Precision.HIG...  29.5 us
    select_n x2, other arithmetic, shards(): window = jnp.take(gathered, picks, axis=0)  16.8 us
    gather x1, local copies, waits for them, and re-layouts, shards(): window = jnp.take(gathered, picks, axis=0)  15.3 us
  transfers between devices with their start and end apart: 3, of which 2 were waited for; matrix products, arithmetic and copies ran while one was open for 7% of the time, Pallas kernels for 0%

commit v1 on v0

v1 whole, which is shorter than its diff:
```python
import functools
import math

import jax
import jax.numpy as jnp
from jax import lax
from jax.experimental import pallas as pl
from jax.experimental.pallas import tpu as pltpu
from jax.sharding import PartitionSpec as P

MODES = 3
REACH = 2
MESH = pl.DeviceIdType.MESH
F32, BF16 = jnp.float32, jnp.bfloat16


def split(x):
    high = x.astype(BF16)
    return high, (x - high.astype(F32)).astype(BF16)


def dot(x, y):
    return jnp.dot(x, y, preferred_element_type=F32)


def dot3(x, y):
    return dot(x[0], y[0]) + (dot(x[0], y[1]) + dot(x[1], y[0]))


def kernel(
    sizes, green, coup, occ, offs, owners, res,
    grid, raw, mine, theirs, table, cth, ctl, cah, cal, part,
    raw_sem, tab_sem, tab_send, tab_recv, k_send, k_recv,
    z_send, z_recv, s_send, s_recv, o_sem, o_send, o_recv,
):
    ne, na, nk, chunks = sizes
    mom, edev, brows, order = green.shape
    rows_table = coup.shape[0]
    momenta = mom * nk
    line = ne <= 2 * REACH
    slots = ne if line else 2 * REACH + 1
    hops = ne - 1 if line else REACH
    half = brows // nk
    ce = edev // chunks
    emine = edev // nk
    rows_out = order // (na * nk)
    p, a, k = (lax.axis_index(n) for n in ("energy", "atom", "kz"))
    right, left = lax.rem(p + 1, ne), lax.rem(p + ne - 1, ne)

    def when(condition, action):
        if line:
            pl.when(condition)(action)
        else:
            action()

    def raw_copy(c):
        es = pl.ds(c * ce, ce)
        return pltpu.make_async_copy(green.at[:, es], raw.at[:, es], raw_sem.at[c])

    for c in range(chunks):
        raw_copy(c).start()
    tab_local = pltpu.make_async_copy(coup, table.at[pl.ds(a * rows_table, rows_table)], tab_sem)
    tab_local.start()

    barrier = pltpu.get_barrier_semaphore()

    def greet(where):
        pl.semaphore_signal(barrier, inc=1, device_id=where, device_id_type=MESH)

    when(p + 1 < ne, lambda: greet({"energy": right}))
    when(p >= 1, lambda: greet({"energy": left}))
    me = a * nk + k
    peers = na * nk

    def peer(j):
        q = lax.rem(me + j, peers)
        return q, {"atom": q // nk, "kz": lax.rem(q, nk)}

    for j in range(1, peers):
        greet(peer(j)[1])
    if line:
        beside = jnp.where(p + 1 < ne, 1, 0) + jnp.where(p >= 1, 1, 0)
    else:
        beside = 2
    pl.semaphore_wait(barrier, peers - 1 + beside)

    def remote(src, dst, send, recv, where):
        return pltpu.make_async_remote_copy(
            src_ref=src, dst_ref=dst, send_sem=send, recv_sem=recv,
            device_id=where, device_id_type=MESH,
        )

    def tab_copy(j):
        return remote(
            coup, table.at[pl.ds(a * rows_table, rows_table)], tab_send.at[j - 1], tab_recv.at[j - 1],
            {"atom": lax.rem(a + j, na)},
        )

    def tab_arrival(j):
        source = lax.rem(a + na - j, na)
        return remote(
            coup, table.at[pl.ds(source * rows_table, rows_table)], tab_send.at[j - 1], tab_recv.at[j - 1],
            {"atom": lax.rem(a + j, na)},
        )

    def k_copy(j, c):
        es = pl.ds(c * ce, ce)
        return remote(
            mine.at[es], theirs.at[j - 1, es], k_send.at[j - 1, c], k_recv.at[j - 1, c],
            {"kz": lax.rem(k + j, nk)},
        )

    my_rows = pl.ds(pl.multiple_of(k * half, half), half)

    def z_copy(d, h, c):
        s, t = ((slots - h + 1) % slots, (slots - h) % slots) if d == 0 else (h - 1, h)
        return remote(
            grid.at[pl.ds(s * edev + c * ce, ce), my_rows], grid.at[pl.ds(t * edev + c * ce, ce), my_rows],
            z_send.at[d, h - 1, c], z_recv.at[d, h - 1, c], {"energy": right if d == 0 else left},
        )

    def sends(d, h):
        if d == 0:
            return jnp.logical_and(p - h + 1 >= 0, p + 1 < ne)
        return jnp.logical_and(p + h - 1 < ne, p >= 1)

    def receives(d, h):
        return p - h >= 0 if d == 0 else p + h < ne

    def share_copy(j, d, h, c, rows):
        t = (slots - h) % slots if d == 0 else h
        at = grid.at[pl.ds(t * edev + c * ce, ce), rows]
        return remote(
            at, at, s_send.at[j - 1, d, h - 1, c], s_recv.at[j - 1, d, h - 1, c],
            {"kz": lax.rem(k + j, nk)},
        )

    def share_arrival(j, d, h, c):
        source = lax.rem(k + nk - j, nk)
        return share_copy(j, d, h, c, pl.ds(pl.multiple_of(source * half, half), half))

    for j in range(1, na):
        tab_copy(j).start()
    for c in range(chunks):
        raw_copy(c).wait()
        for e in range(c * ce, (c + 1) * ce):
            total = raw[0, e]
            for i in range(1, mom):
                total = total + raw[i, e]
            mine[e] = total
        for j in range(1, nk):
            k_copy(j, c).start()
    for c in range(chunks):
        for j in range(1, nk):
            k_copy(j, c).wait_recv()
        for e in range(c * ce, (c + 1) * ce):
            total = mine[e]
            for j in range(1, nk):
                total = total + theirs[j - 1, e]
            grid[e] = total
        for d in range(2):
            when(sends(d, 1), lambda d=d, c=c: z_copy(d, 1, c).start())

    tab_local.wait()
    for j in range(1, na):
        tab_arrival(j).wait_recv()
    for m in range(MODES):
        owner = owners[m]
        high, low = split(table[owner].T)
        cth[m] = high
        ctl[m] = low
        high, low = split(table[owner, :, pl.ds(pl.multiple_of(a * brows, brows), brows)])
        cah[m] = high
        cal[m] = low

    for h in range(1, hops + 1):
        for c in range(chunks):
            for d in range(2):

                def arrived(d=d, h=h, c=c):
                    z_copy(d, h, c).wait_recv()
                    for j in range(1, nk):
                        share_copy(j, d, h, c, my_rows).start()

                when(receives(d, h), arrived)
                if h < hops:
                    when(sends(d, h + 1), lambda d=d, h=h, c=c: z_copy(d, h + 1, c).start())
    for h in range(1, hops + 1):
        for c in range(chunks):
            for d in range(2):
                for j in range(1, nk):
                    when(receives(d, h), lambda j=j, d=d, h=h, c=c: share_arrival(j, d, h, c).wait_recv())

    span = slots * edev

    def o_copy(j, i):
        q, where = peer(j)
        return remote(
            part.at[i, pl.ds(pl.multiple_of(q * rows_out, rows_out), rows_out)], res.at[me, i],
            o_send.at[j - 1, i], o_recv.at[j - 1, i], where,
        )

    def o_arrival(j, i):
        source = lax.rem(me + peers - j, peers)
        return remote(
            part.at[i, pl.ds(0, rows_out)], res.at[source, i],
            o_send.at[j - 1, i], o_recv.at[j - 1, i], peer(j)[1],
        )

    def o_local(i):
        return pltpu.make_async_copy(
            part.at[i, pl.ds(pl.multiple_of(me * rows_out, rows_out), rows_out)], res.at[me, i], o_sem.at[i]
        )

    for i in range(emine):
        e = k * emine + i
        for m in range(MODES):
            weight, step = occ[m], offs[m]
            upper = grid[lax.rem(e + step, span)]
            lower = grid[lax.rem(e - step + span, span)]
            combined = ((1.0 + weight) * upper + weight * lower) / momenta
            product = dot3(split(combined), (cth[m], ctl[m]))
            term = dot3((cah[m], cal[m]), split(product))
            if m == 0:
                part[i] = term
            else:
                part[i] += term
        for j in range(1, peers):
            o_copy(j, i).start()
        o_local(i).start()

    for j in range(1, na):
        tab_copy(j).wait_send()
    for c in range(chunks):
        for j in range(1, nk):
            k_copy(j, c).wait_send()
        for h in range(1, hops + 1):
            for d in range(2):
                when(sends(d, h), lambda d=d, h=h, c=c: z_copy(d, h, c).wait_send())
                for j in range(1, nk):
                    when(receives(d, h), lambda j=j, d=d, h=h, c=c: share_copy(j, d, h, c, my_rows).wait_send())
    for i in range(emine):
        o_local(i).wait()
        for j in range(1, peers):
            o_copy(j, i).wait_send()
            o_arrival(j, i).wait_recv()


def shards(green, couplings, occupation, offsets, owners):
    mom, edev, brows, order = green.shape
    ne, na, nk = (lax.axis_size(n) for n in ("energy", "atom", "kz"))
    chunks = math.gcd(edev, 4)
    line = ne <= 2 * REACH
    slots = ne if line else 2 * REACH + 1
    hops = ne - 1 if line else REACH
    emine, rows_out = edev // nk, order // (na * nk)
    dma = pltpu.SemaphoreType.DMA
    smem = pl.BlockSpec(memory_space=pltpu.SMEM)
    hbm = pl.BlockSpec(memory_space=pl.ANY)
    parts = pl.pallas_call(
        functools.partial(kernel, (ne, na, nk, chunks)),
        out_shape=jax.ShapeDtypeStruct((na * nk, emine, rows_out, order), F32),
        in_specs=[hbm, hbm, smem, smem, smem],
        out_specs=hbm,
        scratch_shapes=[
            pltpu.VMEM((slots * edev, brows, order), F32),
            pltpu.VMEM((mom, edev, brows, order), F32),
            pltpu.VMEM((edev, brows, order), F32),
            pltpu.VMEM((nk - 1, edev, brows, order), F32),
            pltpu.VMEM((couplings.shape[0] * na, order, order), F32),
            pltpu.VMEM((MODES, order, order), BF16),
            pltpu.VMEM((MODES, order, order), BF16),
            pltpu.VMEM((MODES, order, brows), BF16),
            pltpu.VMEM((MODES, order, brows), BF16),
            pltpu.VMEM((emine, order, order), F32),
            dma((chunks,)),
            dma,
            dma((na - 1,)),
            dma((na - 1,)),
            dma((nk - 1, chunks)),
            dma((nk - 1, chunks)),
            dma((2, hops, chunks)),
            dma((2, hops, chunks)),
            dma((nk - 1, 2, hops, chunks)),
            dma((nk - 1, 2, hops, chunks)),
            dma((emine,)),
            dma((na * nk - 1, emine)),
            dma((na * nk - 1, emine)),
        ],
        compiler_params=pltpu.CompilerParams(
            collective_id=0, has_side_effects=True, vmem_limit_bytes=58 << 20
        ),
        cost_estimate=pl.CostEstimate(
            flops=12 * MODES * emine * 2 * brows * order * order,
            bytes_accessed=4 * (mom * edev * brows * order + couplings.size + na * nk * emine * rows_out * order),
            transcendentals=0,
        ),
    )(green, couplings, occupation, offsets, owners)
    sigma = jnp.sum(parts.reshape(na, edev, rows_out, order), axis=0)
    return jnp.swapaxes(sigma, 0, 1)


def solution(mesh):
    return jax.shard_map(
        shards,
        mesh=mesh,
        in_specs=(P(("grp", "kz"), "energy", "atom", None), P("atom", None, None), P(), P(), P()),
        out_specs=P(("grp", "atom", "kz"), "energy", None),
        check_vma=False,
    )
```

time: 478 us -> 202 us (0.42)
  waiting for transfers between devices: 338 us -> 0 us
  Pallas kernels: 0 us -> 194 us
  matrix products: 60.1 us -> 0 us
  between operations: 32.4 us -> 0.02 us
  other arithmetic: 25.4 us -> 2.87 us
  local copies, waits for them, and re-layouts: 21.9 us -> 2.54 us
    all_gather x1 -> x0, waiting for transfers between devices: 268 us -> none  [shards(): gathered = lax.all_gather(source, 'energy', axis=0, tiled=True)]
    pallas_call x0 -> x1, Pallas kernels: none -> 194 us  [shards(): pl.pallas_call(functools.partial(kernel, (ne, na, nk, chunks)), out_shape...]
    reduce_scatter x1 -> x0, waiting for transfers between devices: 69.9 us -> none  [shards(): lax.psum_scatter(total, ('atom', 'kz'), scatter_dimension=0, tiled=True)]
    dot_general x6 -> x0, matrix products: 60.1 us -> none  [the longest x3 30.5 us: shards(): jnp.einsum('ra,ead->red', block, product, precision=lax.Precision.HIGHEST)]
    select_n x3 -> x0, other arithmetic: 18.5 us -> none  [the longest x2 16.8 us: shards(): window = jnp.take(gathered, picks, axis=0)]
    gather x1 -> x0, local copies, waits for them, and re-layouts: 15.3 us -> none  [shards(): window = jnp.take(gathered, picks, axis=0)]
  transfers between devices with their start and end apart: 3 -> 0, of which waited for: 2 -> 0; matrix products, arithmetic and copies ran while one was open for 7% -> 0% of each run, Pallas kernels for 0% -> 0%
where the time goes in v1:
time: 202 us; the launch traced here: 199 us
  Pallas kernels  194 us (96%)
  other arithmetic  2.87 us (1%)
  local copies, waits for them, and re-layouts  2.54 us (1%)
    pallas_call x1, Pallas kernels, shards(): pl.pallas_call(functools.partial(kernel, (ne, na, nk, chunks)), out_shape...  194 us

profile of v1, /device:TPU:0, one launch (start us, length us, event | category | flops | bytes accessed | tf_op | source)
XLA Modules:
  0.0 199.2 jit_solution(2708780166370218216)
XLA Ops:
  0.0 193.8 %shard_map.55 = f32[4,4,128,512]{3,2,1,0:T(8,128)} custom-call(f32[2,8,256,512]{3,2,1,0:T(8,128)} %green.1, f32[2,512,512]{2,1,0:T(8,128)} %coup.1, f32[3]{0:T(128)} %occ.1, s32[3]{0:T(128)} %offs.1, s32[3]{0:T(128)} %owners.1), custom_call_target="tpu_custom_call" | custom-call | flops 19327352832 | bytes 14680064 | tf_op jit(solution)/shard_map/pallas_call | solution.py:260
  193.8 2.9 %bitcast_reduce_fusion = f32[8,128,512]{2,1,0:T(8,128)S(1)} fusion(f32[2,8,128,512]{3,2,1,0:T(8,128)} %bitcast.5), kind=kLoop, calls=%fused_computation | loop fusion | flops 524288 | bytes 6291456 | tf_op jit(solution)/shard_map/reduce_sum | solution.py:299
  196.7 2.5 %copy.6 = f32[128,8,512]{2,1,0:T(8,128)} copy(f32[128,8,512]{2,0,1:T(8,128)S(1)} %bitcast.4) | data formatting | bytes 4194304 | tf_op jit(solution)/shard_map/transpose | solution.py:300

commit v2 on v1

--- a/solution.py
+++ b/solution.py
@@ -29,9 +29,10 @@
 
 def kernel(
     sizes, green, coup, occ, offs, owners, res,
-    grid, raw, mine, theirs, table, cth, ctl, cah, cal, part,
+    grid, raw, mine, theirs, table, cth, ctl, cah, cal, part, other, crh, crl, fpart,
     raw_sem, tab_sem, tab_send, tab_recv, k_send, k_recv,
     z_send, z_recv, s_send, s_recv, o_sem, o_send, o_recv,
+    x_send, x_recv, xs_send, xs_recv, f_send, f_recv,
 ):
     ne, na, nk, chunks = sizes
     mom, edev, brows, order = green.shape
@@ -39,13 +40,17 @@
     momenta = mom * nk
     line = ne <= 2 * REACH
     slots = ne if line else 2 * REACH + 1
-    hops = ne - 1 if line else REACH
+    hops = min(ne - 1, REACH)
+    far = line and ne - 1 > REACH
     half = brows // nk
     ce = edev // chunks
     emine = edev // nk
     rows_out = order // (na * nk)
     p, a, k = (lax.axis_index(n) for n in ("energy", "atom", "kz"))
     right, left = lax.rem(p + 1, ne), lax.rem(p + ne - 1, ne)
+    beside_end = jnp.logical_and(p >= 1, p + 1 < ne)
+    at_end = jnp.logical_or(p < 1, p + 1 >= ne)
+    partner = lax.rem((ne - 1) * (p - 1) + ne * ne, ne)
 
     def when(condition, action):
         if line:
@@ -82,6 +87,10 @@
         beside = jnp.where(p + 1 < ne, 1, 0) + jnp.where(p >= 1, 1, 0)
     else:
         beside = 2
+    if far:
+        for j in range(1, nk):
+            greet({"energy": partner, "kz": lax.rem(k + j, nk)})
+        beside = beside + nk - 1
     pl.semaphore_wait(barrier, peers - 1 + beside)
 
     def remote(src, dst, send, recv, where):
@@ -138,6 +147,27 @@
     def share_arrival(j, d, h, c):
         source = lax.rem(k + nk - j, nk)
         return share_copy(j, d, h, c, pl.ds(pl.multiple_of(source * half, half), half))
+
+    def x_copy(j, c):
+        return remote(
+            grid.at[pl.ds(REACH * edev + c * ce, ce), my_rows], other.at[j - 1, pl.ds(c * ce, ce), my_rows],
+            x_send.at[j - 1, c], x_recv.at[j - 1, c], {"atom": lax.rem(a + j, na)},
+        )
+
+    def xs_copy(j, i, c, rows):
+        at = other.at[j - 1, pl.ds(c * ce, ce), rows]
+        return remote(
+            at, at, xs_send.at[j - 1, i - 1, c], xs_recv.at[j - 1, i - 1, c], {"kz": lax.rem(k + i, nk)}
+        )
+
+    def xs_arrival(j, i, c):
+        source = lax.rem(k + nk - i, nk)
+        return xs_copy(j, i, c, pl.ds(pl.multiple_of(source * half, half), half))
+
+    def far_here(d):
+        if d == 0:
+            return jnp.logical_and(p >= REACH, p + 1 < ne)
+        return jnp.logical_and(p + REACH < ne, p >= 1)
 
     for j in range(1, na):
         tab_copy(j).start()
@@ -172,6 +202,13 @@
         high, low = split(table[owner, :, pl.ds(pl.multiple_of(a * brows, brows), brows)])
         cah[m] = high
         cal[m] = low
+        if far:
+            for j in range(na):
+                columns = pl.ds(pl.multiple_of(lax.rem(a + na - j, na) * brows, brows), brows)
+                rows = pl.ds(pl.multiple_of(a * brows, brows), brows)
+                high, low = split(table[owner, rows, columns])
+                crh[m * na + j] = high
+                crl[m * na + j] = low
 
     for h in range(1, hops + 1):
         for c in range(chunks):
@@ -183,8 +220,25 @@
                         share_copy(j, d, h, c, my_rows).start()
 
                 when(receives(d, h), arrived)
+                if far and h == hops:
+
+                    def spread(c=c):
+                        for j in range(1, na):
+                            x_copy(j, c).start()
+
+                    pl.when(far_here(d))(spread)
                 if h < hops:
                     when(sends(d, h + 1), lambda d=d, h=h, c=c: z_copy(d, h + 1, c).start())
+    if far:
+
+        @pl.when(beside_end)
+        def _():
+            for c in range(chunks):
+                for j in range(1, na):
+                    x_copy(j, c).wait_recv()
+                    for i in range(1, nk):
+                        xs_copy(j, i, c, my_rows).start()
+
     for h in range(1, hops + 1):
         for c in range(chunks):
             for d in range(2):
@@ -212,13 +266,35 @@
             part.at[i, pl.ds(pl.multiple_of(me * rows_out, rows_out), rows_out)], res.at[me, i], o_sem.at[i]
         )
 
-    for i in range(emine):
+    def f_copy(j, i):
+        q = lax.rem(k + j, nk)
+        return remote(
+            fpart.at[i, pl.ds(pl.multiple_of(q * rows_out, rows_out), rows_out)], res.at[peers + k, i],
+            f_send.at[j, i], f_recv.at[j, i], {"energy": partner, "kz": q},
+        )
+
+    def f_arrival(j, i):
+        return remote(
+            fpart.at[i, pl.ds(0, rows_out)], res.at[peers + lax.rem(k + nk - j, nk), i],
+            f_send.at[j, i], f_recv.at[j, i], {"energy": partner, "kz": lax.rem(k + j, nk)},
+        )
+
+    if far:
+        missing = jnp.where(p < 1, slots - 1, jnp.where(p + 1 >= ne, 1, -1))
+
+    def seen(index, e, weight):
+        if not far:
+            return index, weight
+        absent = lax.div(index, edev) == missing
+        return jnp.where(absent, e, index), jnp.where(absent, 0.0, weight)
+
+    def near(i):
         e = k * emine + i
         for m in range(MODES):
             weight, step = occ[m], offs[m]
-            upper = grid[lax.rem(e + step, span)]
-            lower = grid[lax.rem(e - step + span, span)]
-            combined = ((1.0 + weight) * upper + weight * lower) / momenta
+            iu, wu = seen(lax.rem(e + step, span), e, 1.0 + weight)
+            il, wl = seen(lax.rem(e - step + span, span), e, weight)
+            combined = (wu * grid[iu] + wl * grid[il]) / momenta
             product = dot3(split(combined), (cth[m], ctl[m]))
             term = dot3((cah[m], cal[m]), split(product))
             if m == 0:
@@ -228,6 +304,46 @@
         for j in range(1, peers):
             o_copy(j, i).start()
         o_local(i).start()
+
+    def among(index, weight):
+        inside = index < edev
+        return jnp.where(inside, index, 0), jnp.where(inside, weight, 0.0)
+
+    def farthest(i):
+        e = (ne - 1) * (2 * p - ne + 1) * edev + span + k * emine + i
+        for m in range(MODES):
+            weight, step = occ[m], offs[m]
+            iu, wu = among(lax.rem(e + step, span), 1.0 + weight)
+            il, wl = among(lax.rem(e - step + span, span), weight)
+            rows = None
+            for j in range(na):
+                if j == 0:
+                    upper, lower = grid[REACH * edev + iu], grid[REACH * edev + il]
+                else:
+                    upper, lower = other[j - 1, iu], other[j - 1, il]
+                combined = (wu * upper + wl * lower) / momenta
+                term = dot3((crh[m * na + j], crl[m * na + j]), split(combined))
+                rows = term if rows is None else rows + term
+            term = dot3(split(rows), (cth[m], ctl[m]))
+            if m == 0:
+                fpart[i] = term
+            else:
+                fpart[i] += term
+        for j in range(nk):
+            f_copy(j, i).start()
+
+    for i in range(emine):
+        near(i)
+        if far:
+
+            @pl.when(beside_end)
+            def _():
+                if i == 0:
+                    for c in range(chunks):
+                        for j in range(1, na):
+                            for t in range(1, nk):
+                                xs_arrival(j, t, c).wait_recv()
+                farthest(i)
 
     for j in range(1, na):
         tab_copy(j).wait_send()
@@ -239,6 +355,25 @@
                 when(sends(d, h), lambda d=d, h=h, c=c: z_copy(d, h, c).wait_send())
                 for j in range(1, nk):
                     when(receives(d, h), lambda j=j, d=d, h=h, c=c: share_copy(j, d, h, c, my_rows).wait_send())
+    if far:
+
+        @pl.when(beside_end)
+        def _():
+            for c in range(chunks):
+                for j in range(1, na):
+                    x_copy(j, c).wait_send()
+                    for i in range(1, nk):
+                        xs_copy(j, i, c, my_rows).wait_send()
+            for i in range(emine):
+                for j in range(nk):
+                    f_copy(j, i).wait_send()
+
+        @pl.when(at_end)
+        def _():
+            for i in range(emine):
+                for j in range(nk):
+                    f_arrival(j, i).wait_recv()
+
     for i in range(emine):
         o_local(i).wait()
         for j in range(1, peers):
@@ -252,14 +387,18 @@
     chunks = math.gcd(edev, 4)
     line = ne <= 2 * REACH
     slots = ne if line else 2 * REACH + 1
-    hops = ne - 1 if line else REACH
+    hops = min(ne - 1, REACH)
     emine, rows_out = edev // nk, order // (na * nk)
+    far = line and ne - 1 > REACH
+    extra = nk if far else 0
+    f_edev, f_emine, f_brows = (edev, emine, brows) if far else (8, 8, 128)
+    f_modes = MODES if far else 1
     dma = pltpu.SemaphoreType.DMA
     smem = pl.BlockSpec(memory_space=pltpu.SMEM)
     hbm = pl.BlockSpec(memory_space=pl.ANY)
     parts = pl.pallas_call(
         functools.partial(kernel, (ne, na, nk, chunks)),
-        out_shape=jax.ShapeDtypeStruct((na * nk, emine, rows_out, order), F32),
+        out_shape=jax.ShapeDtypeStruct((na * nk + extra, emine, rows_out, order), F32),
         in_specs=[hbm, hbm, smem, smem, smem],
         out_specs=hbm,
         scratch_shapes=[
@@ -273,6 +412,10 @@
             pltpu.VMEM((MODES, order, brows), BF16),
             pltpu.VMEM((MODES, order, brows), BF16),
             pltpu.VMEM((emine, order, order), F32),
+            pltpu.VMEM((na - 1, f_edev, f_brows, order if far else 128), F32),
+            pltpu.VMEM((f_modes * na, f_brows, f_brows), BF16),
+            pltpu.VMEM((f_modes * na, f_brows, f_brows), BF16),
+            pltpu.VMEM((f_emine, f_brows, order if far else 128), F32),
             dma((chunks,)),
             dma,
             dma((na - 1,)),
@@ -286,6 +429,12 @@
             dma((emine,)),
             dma((na * nk - 1, emine)),
             dma((na * nk - 1, emine)),
+            dma((na - 1, chunks)),
+            dma((na - 1, chunks)),
+            dma((na - 1, nk - 1, chunks)),
+            dma((na - 1, nk - 1, chunks)),
+            dma((nk, emine)),
+            dma((nk, emine)),
         ],
         compiler_params=pltpu.CompilerParams(
             collective_id=0, has_side_effects=True, vmem_limit_bytes=58 << 20
@@ -296,7 +445,11 @@
             transcendentals=0,
         ),
     )(green, couplings, occupation, offsets, owners)
-    sigma = jnp.sum(parts.reshape(na, edev, rows_out, order), axis=0)
+    sigma = jnp.sum(parts[: na * nk].reshape(na, edev, rows_out, order), axis=0)
+    if far:
+        place = lax.axis_index("energy")
+        end = jnp.logical_or(place == 0, place == ne - 1)
+        sigma = sigma + jnp.where(end, parts[na * nk :].reshape(edev, rows_out, order), 0.0)
     return jnp.swapaxes(sigma, 0, 1)
 
 

time: 202 us -> 173 us (0.86)
  Pallas kernels: 194 us -> 163 us
  local copies, waits for them, and re-layouts: 2.54 us -> 4.72 us
    pallas_call x1, Pallas kernels: 194 us -> 163 us  [shards(): pl.pallas_call(functools.partial(kernel, (ne, na, nk, chunks)), out_shape...]
    reduce_sum x1, other arithmetic: 2.87 us -> 0.53 us  [shards(): sigma = jnp.sum(parts[:na * nk].reshape(na, edev, rows_out, order), axis=0)]
    slice x0 -> x2, local copies, waits for them, and re-layouts: none -> 2.18 us  [shards(): sigma = jnp.sum(parts[:na * nk].reshape(na, edev, rows_out, order), axis=0)]
where the time goes in v2:
time: 173 us; the launch traced here: 171 us
  Pallas kernels  163 us (94%)
  local copies, waits for them, and re-layouts  4.72 us (3%)
  other arithmetic  2.98 us (2%)
    pallas_call x1, Pallas kernels, shards(): pl.pallas_call(functools.partial(kernel, (ne, na, nk, chunks)), out_shape...  163 us

profile of v2, /device:TPU:0, one launch (start us, length us, event | category | flops | bytes accessed | tf_op | source)
XLA Modules:
  0.0 171.1 jit_solution(15844861498943360403)
XLA Ops:
  0.0 163.4 %shard_map.55 = f32[6,4,128,512]{3,2,1,0:T(8,128)} custom-call(f32[2,8,256,512]{3,2,1,0:T(8,128)} %green.1, f32[2,512,512]{2,1,0:T(8,128)} %coup.1, f32[3]{0:T(128)} %occ.1, s32[3]{0:T(128)} %offs.1, s32[3]{0:T(128)} %owners.1), custom_call_target="tpu_custom_call" | custom-call | flops 19327352832 | bytes 14680064 | tf_op jit(solution)/shard_map/pallas_call | solution.py:399
  163.4 2.0 %slice_select_fusion = f32[2,4,128,512]{3,2,1,0:T(8,128)S(1)} fusion(f32[6,4,128,512]{3,2,1,0:T(8,128)} %shard_map.55, pred[]{:T(512)S(6)} %or.3), kind=kLoop, calls=%fused_computation.2 | loop fusion | flops 524288 | bytes 4194305 | tf_op jit(solution)/shard_map/jit(_where)/select_n | solution.py:452
  165.4 0.0 slice-start
  165.4 2.2 %slice-done = f32[4,4,128,512]{3,2,1,0:T(8,128)S(1)} async-done(((f32[6,4,128,512]{3,2,1,0:T(8,128)}), f32[4,4,128,512]{3,2,1,0:T(8,128)S(1)}, s32[]{:S(2)}) %slice-start) | async-done | bytes 4194328 | tf_op jit(solution)/shard_map/slice | solution.py:448
  167.6 0.5 bitcast_reduce_fusion
  168.1 0.5 bitcast_add_fusion
  168.6 2.5 %copy.7 = f32[128,8,512]{2,1,0:T(8,128)} copy(f32[128,8,512]{2,0,1:T(8,128)S(1)} %bitcast.7) | data formatting | bytes 4194304 | tf_op jit(solution)/shard_map/transpose | solution.py:453
Async XLA Ops:
  165.4 2.2 %slice-start = ((f32[6,4,128,512]{3,2,1,0:T(8,128)}), f32[4,4,128,512]{3,2,1,0:T(8,128)S(1)}, s32[]{:S(2)}) async-start(f32[6,4,128,512]{3,2,1,0:T(8,128)} %shard_map.55), calls=%async_computation | async-start | bytes 8388608 | tf_op jit(solution)/shard_map/slice | solution.py:448

commit v3 on v2

--- a/solution.py
+++ b/solution.py
@@ -28,7 +28,7 @@
 
 
 def kernel(
-    sizes, green, coup, occ, offs, owners, res,
+    sizes, green, coup, occ, offs, owners, res, ends,
     grid, raw, mine, theirs, table, cth, ctl, cah, cal, part, other, crh, crl, fpart,
     raw_sem, tab_sem, tab_send, tab_recv, k_send, k_recv,
     z_send, z_recv, s_send, s_recv, o_sem, o_send, o_recv,
@@ -231,13 +231,15 @@
                     when(sends(d, h + 1), lambda d=d, h=h, c=c: z_copy(d, h + 1, c).start())
     if far:
 
-        @pl.when(beside_end)
-        def _():
-            for c in range(chunks):
+        def pass_on(first, last):
+            for c in range(first, last):
                 for j in range(1, na):
                     x_copy(j, c).wait_recv()
                     for i in range(1, nk):
                         xs_copy(j, i, c, my_rows).start()
+
+        late = max(chunks - 2, 0)
+        pl.when(beside_end)(lambda: pass_on(0, late))
 
     for h in range(1, hops + 1):
         for c in range(chunks):
@@ -269,13 +271,13 @@
     def f_copy(j, i):
         q = lax.rem(k + j, nk)
         return remote(
-            fpart.at[i, pl.ds(pl.multiple_of(q * rows_out, rows_out), rows_out)], res.at[peers + k, i],
+            fpart.at[i, pl.ds(pl.multiple_of(q * rows_out, rows_out), rows_out)], ends.at[k, i],
             f_send.at[j, i], f_recv.at[j, i], {"energy": partner, "kz": q},
         )
 
     def f_arrival(j, i):
         return remote(
-            fpart.at[i, pl.ds(0, rows_out)], res.at[peers + lax.rem(k + nk - j, nk), i],
+            fpart.at[i, pl.ds(0, rows_out)], ends.at[lax.rem(k + nk - j, nk), i],
             f_send.at[j, i], f_recv.at[j, i], {"energy": partner, "kz": lax.rem(k + j, nk)},
         )
 
@@ -339,6 +341,7 @@
             @pl.when(beside_end)
             def _():
                 if i == 0:
+                    pass_on(late, chunks)
                     for c in range(chunks):
                         for j in range(1, na):
                             for t in range(1, nk):
@@ -384,23 +387,25 @@
 def shards(green, couplings, occupation, offsets, owners):
     mom, edev, brows, order = green.shape
     ne, na, nk = (lax.axis_size(n) for n in ("energy", "atom", "kz"))
-    chunks = math.gcd(edev, 4)
+    chunks = math.gcd(edev, 8)
     line = ne <= 2 * REACH
     slots = ne if line else 2 * REACH + 1
     hops = min(ne - 1, REACH)
     emine, rows_out = edev // nk, order // (na * nk)
     far = line and ne - 1 > REACH
-    extra = nk if far else 0
     f_edev, f_emine, f_brows = (edev, emine, brows) if far else (8, 8, 128)
     f_modes = MODES if far else 1
     dma = pltpu.SemaphoreType.DMA
     smem = pl.BlockSpec(memory_space=pltpu.SMEM)
     hbm = pl.BlockSpec(memory_space=pl.ANY)
-    parts = pl.pallas_call(
+    parts, finished = pl.pallas_call(
         functools.partial(kernel, (ne, na, nk, chunks)),
-        out_shape=jax.ShapeDtypeStruct((na * nk + extra, emine, rows_out, order), F32),
+        out_shape=(
+            jax.ShapeDtypeStruct((na * nk, emine, rows_out, order), F32),
+            jax.ShapeDtypeStruct((nk, emine, rows_out, order) if far else (8, 128), F32),
+        ),
         in_specs=[hbm, hbm, smem, smem, smem],
-        out_specs=hbm,
+        out_specs=(hbm, hbm),
         scratch_shapes=[
             pltpu.VMEM((slots * edev, brows, order), F32),
             pltpu.VMEM((mom, edev, brows, order), F32),
@@ -445,11 +450,11 @@
             transcendentals=0,
         ),
     )(green, couplings, occupation, offsets, owners)
-    sigma = jnp.sum(parts[: na * nk].reshape(na, edev, rows_out, order), axis=0)
+    sigma = jnp.sum(parts.reshape(na, edev, rows_out, order), axis=0)
     if far:
         place = lax.axis_index("energy")
         end = jnp.logical_or(place == 0, place == ne - 1)
-        sigma = sigma + jnp.where(end, parts[na * nk :].reshape(edev, rows_out, order), 0.0)
+        sigma = sigma + jnp.where(end, finished.reshape(edev, rows_out, order), 0.0)
     return jnp.swapaxes(sigma, 0, 1)
 
 

time: 173 us -> 167 us (0.965); the launches traced: 171 us -> 167 us
  Pallas kernels: 163 us -> 159 us
  other arithmetic: 2.98 us -> 5.18 us
  local copies, waits for them, and re-layouts: 4.72 us -> 2.54 us
    pallas_call x1, Pallas kernels: 163 us -> 159 us  [shards(): pl.pallas_call(functools.partial(kernel, (ne, na, nk, chunks)), out_shape...]
    reduce_sum x1, other arithmetic: 0.53 us -> 2.87 us  [shards(): sigma = jnp.sum(parts.reshape(na, edev, rows_out, order), axis=0)]
    slice x2 -> x0, local copies, waits for them, and re-layouts: 2.18 us -> none  [shards(): sigma = jnp.sum(parts[:na * nk].reshape(na, edev, rows_out, order), axis=0)]
where the time goes in v3:
time: 167 us
  Pallas kernels  159 us (95%)
  other arithmetic  5.18 us (3%)
  local copies, waits for them, and re-layouts  2.54 us (2%)
    pallas_call x1, Pallas kernels, shards(): pl.pallas_call(functools.partial(kernel, (ne, na, nk, chunks)), out_shape...  159 us

profile of v3, /device:TPU:0, one launch (start us, length us, event | category | flops | bytes accessed | tf_op | source)
XLA Modules:
  0.0 167.2 jit_solution(15247907903063914494)
XLA Ops:
  0.0 159.5 %shard_map.55 = (f32[4,4,128,512]{3,2,1,0:T(8,128)}, f32[2,4,128,512]{3,2,1,0:T(8,128)}) custom-call(f32[2,8,256,512]{3,2,1,0:T(8,128)} %green.1, f32[2,512,512]{2,1,0:T(8,128)} %coup.1, f32[3]{0:T(128)} %occ.1, s32[3]{0:T(128)} %offs.1, s32[3]{0:T(128)} %owners.1), custom_call_target="tpu_custom_call" | custom-call | flops 19327352832 | bytes 14680064 | tf_op jit(solution)/shard_map/pallas_call | solution.py:401
  159.5 2.9 %bitcast_reduce_fusion = f32[8,128,512]{2,1,0:T(8,128)S(1)} fusion(f32[2,8,128,512]{3,2,1,0:T(8,128)} %bitcast.7), kind=kLoop, calls=%fused_computation | loop fusion | flops 524288 | bytes 6291456 | tf_op jit(solution)/shard_map/reduce_sum | solution.py:453
  162.4 1.8 %broadcast_select_fusion = f32[2,4,128,512]{3,2,1,0:T(8,128)S(1)} fusion(f32[2,4,128,512]{3,2,1,0:T(8,128)} %get-tuple-element.8, pred[]{:T(512)S(6)} %or.3), kind=kLoop, calls=%fused_computation.2 | loop fusion | flops 524288 | bytes 4194305 | tf_op jit(solution)/shard_map/jit(_where)/select_n | solution.py:457
  164.2 0.5 bitcast_add_fusion
  164.7 2.5 %copy.7 = f32[128,8,512]{2,1,0:T(8,128)} copy(f32[128,8,512]{2,0,1:T(8,128)S(1)} %bitcast.6) | data formatting | bytes 4194304 | tf_op jit(solution)/shard_map/transpose | solution.py:458
